TPU v7x, 512 devices: a whole 4x4x16 slice. The times are simulated.
512 devices in a mesh: gx: 32 (over z, core), gy: 16 (over y, x).
Axes of the slice: x: 4, y: 4, z: 16, core: 2. Of those that a mesh axis runs over, the one named last changes fastest.
Arguments:
- solution: float32 [512, 65536], P(None, ('gx', 'gy')), may hold values from -6 to 6
- residual: float32 [512, 65536], P(None, ('gx', 'gy')), may hold values from -60 to 60
- metric_diag: bfloat16 [3, 512, 65536], P(None, None, ('gx', 'gy')), may hold values from 0.039794922 to 0.3984375
- metric_cross: bfloat16 [3, 512, 65536], P(None, None, ('gx', 'gy')), may hold values from -0.017944336 to 0.017944336
- fdm_vectors: float32 [3, 8, 8, 65536], P(None, None, None, ('gx', 'gy')), may hold values from -5 to 5
- fdm_values: float32 [3, 8, 65536], P(None, None, ('gx', 'gy')), may hold values from 0.05 to 20
- vertex_ids: int32 [8, 65536], P(None, ('gx', 'gy')), may hold values from 0 to 8191
- coarse_inverse: float32 [8192, 8192], P(('gx', 'gy')), may hold values from -0.2 to 0.2, as said below
- elem_live: int32 [512], P(('gx', 'gy')), may hold values from 80 to 128, as said below
- section_face: int32 [512, 16, 20], P(('gx', 'gy')), may hold values from -1 to 767, as said below
- section_code: int32 [512, 16, 20], P(('gx', 'gy')), may hold values from 0 to 7, as said below
- pipe_face: int32 [512, 2, 64], P(('gx', 'gy')), may hold values from 0 to 767, as said below
- pipe_code: int32 [512, 2, 64], P(('gx', 'gy')), may hold values from 0 to 7, as said below
Outputs:
- solution_out: float32 [512, 65536], P(None, ('gx', 'gy'))
- residual_out: float32 [512, 65536], P(None, ('gx', 'gy'))
- norm_ratio: float32 [1], replicated
Inputs may be any that keep to these rules, and one draw needn't show every extreme that they name: `elem_live`: one device holds all 128 slots in every draw. A face id 6 e + f names face f of slot e of the device, with e below the device's elem_live; no id appears twice on a device over section_face and pipe_face; -1 marks an empty slot, and in each peer's row the slots holding faces come first. Slot (q, c) of device (x, y) holds a face exactly when slot (y, c) of device (x, q) does; in the row q = y they come in pairs (c, c xor 1). Each device's rows for peers y - 1, y + 1 and y + 16 / 2 (mod 16) are full; rows for other peers more than two places away (mod 16) are empty. `section_code`: with inv(o) = o for o < 4 and 4 + 2 (o mod 2) + floor((o mod 4) / 2) for o >= 4, the codes of two paired slots are inv of each other; empty slots hold 0. `pipe_face`: every slot holds a face, as for section_face. `pipe_code`: the codes of two paired slots are inv of each other, as for section_code. `coarse_inverse`: Symmetric.
All inputs are finite; a program needn't handle non-finite values.
Results may differ from a plain program's by a relative error of at most 0.0003.
Values sent between devices are 32-bit elements; how exact they have to be, the bound alone decides.
A program may use at most 64 MiB of HBM per device.

v0:
```python
import jax
import jax.numpy as jnp
from jax import lax
from jax.sharding import PartitionSpec as P

EDGE = 8
top_precision = lax.Precision.HIGHEST


def padded(block, sides, width):
    for axis, dim in sides:
        count = lax.axis_size(axis)
        forward = [(i, i + 1) for i in range(count - 1)]
        forward.append((count - 1, 0))
        backward = [(target, source) for source, target in forward]
        low = lax.ppermute(
            lax.slice_in_dim(block, block.shape[dim] - width, None, axis=dim), axis, forward
        )
        high = lax.ppermute(lax.slice_in_dim(block, 0, width, axis=dim), axis, backward)
        block = jnp.concatenate([low, block, high], axis=dim)
    return block


def node_points():
    node_index = jnp.arange(EDGE).astype(jnp.float32)
    return -jnp.cos(jnp.pi * node_index / (EDGE - 1))


def derivative_matrix():
    points = node_points()
    node_index = jnp.arange(EDGE)
    weights = jnp.where((node_index == 0) | (node_index == EDGE - 1), 2.0, 1.0).astype(jnp.float32)
    parity = jnp.where((node_index[:, None] + node_index[None, :]) % 2 == 0, 1.0, -1.0).astype(
        jnp.float32
    )
    identity = jnp.eye(EDGE, dtype=jnp.float32)
    spacing = points[:, None] - points[None, :] + identity
    offdiag = weights[:, None] / weights[None, :] * parity / spacing * (1.0 - identity)
    return offdiag - jnp.diag(jnp.sum(offdiag, axis=1))


def corner_table():
    points = node_points()
    hat_values = jnp.stack([(1.0 - points) * 0.5, (1.0 + points) * 0.5])
    corner_weights = (
        hat_values[:, None, None, :, None, None]
        * hat_values[None, :, None, None, :, None]
        * hat_values[None, None, :, None, None, :]
    )
    return corner_weights.reshape(8, EDGE**3)


def contract(matrices, element_cube, axis):
    moved = jnp.moveaxis(element_cube, axis, 0)
    total = matrices[0][:, None, None, :] * moved[0][None]
    for index in range(1, EDGE):
        total = total + matrices[index][:, None, None, :] * moved[index][None]
    return jnp.moveaxis(total, 0, axis)


def orient_columns(face_cols, orient_codes):
    face_grid = face_cols.reshape(EDGE, EDGE, -1)
    face_grid = jnp.where((orient_codes % 2 == 1)[None, None, :], face_grid[::-1, :, :], face_grid)
    face_grid = jnp.where(
        (orient_codes // 2 % 2 == 1)[None, None, :], face_grid[:, ::-1, :], face_grid
    )
    face_grid = jnp.where(
        (orient_codes >= 4)[None, None, :], jnp.swapaxes(face_grid, 0, 1), face_grid
    )
    return face_grid.reshape(EDGE * EDGE, -1)


def fdm_solve(element_cube, vectors, values):
    spectral = contract(vectors[0], element_cube, 0)
    spectral = contract(vectors[1], spectral, 1)
    spectral = contract(vectors[2], spectral, 2)
    eigen_sums = (
        values[0][:, None, None, :] + values[1][None, :, None, :] + values[2][None, None, :, :]
    )
    spectral = spectral / eigen_sums
    restored = contract(jnp.swapaxes(vectors[0], 0, 1), spectral, 0)
    restored = contract(jnp.swapaxes(vectors[1], 0, 1), restored, 1)
    return contract(jnp.swapaxes(vectors[2], 0, 1), restored, 2)


def local_operator(field, diag_part, cross_part, derivative):
    element_cube = field.reshape(EDGE, EDGE, EDGE, -1)
    diagonal = diag_part.astype(jnp.float32).reshape(3, EDGE, EDGE, EDGE, -1)
    cross_terms = cross_part.astype(jnp.float32).reshape(3, EDGE, EDGE, EDGE, -1)
    forward = jnp.transpose(derivative)[:, :, None]
    backward = derivative[:, :, None]
    grad_first = contract(forward, element_cube, 0)
    grad_second = contract(forward, element_cube, 1)
    grad_third = contract(forward, element_cube, 2)
    flux_first = (
        diagonal[0] * grad_first + cross_terms[0] * grad_second + cross_terms[1] * grad_third
    )
    flux_second = (
        cross_terms[0] * grad_first + diagonal[1] * grad_second + cross_terms[2] * grad_third
    )
    flux_third = (
        cross_terms[1] * grad_first + cross_terms[2] * grad_second + diagonal[2] * grad_third
    )
    curvature = jnp.sum(
        grad_first * flux_first + grad_second * flux_second + grad_third * flux_third
    ) + jnp.sum(element_cube * element_cube)
    applied = contract(backward, flux_first, 0)
    applied = applied + contract(backward, flux_second, 1)
    applied = applied + contract(backward, flux_third, 2)
    return ((applied + element_cube).reshape(EDGE**3, -1), curvature)


def face_sum(field, section_face, section_code, pipe_face, pipe_code):
    element_cube = field.reshape(EDGE, EDGE, EDGE, -1)
    slot_count = element_cube.shape[3]
    stacked = jnp.stack(
        [
            element_cube[0],
            element_cube[EDGE - 1],
            element_cube[:, 0],
            element_cube[:, EDGE - 1],
            element_cube[:, :, 0],
            element_cube[:, :, EDGE - 1],
        ],
        axis=-1,
    )
    face_values = stacked.reshape(EDGE * EDGE, slot_count * 6)
    face_count = face_values.shape[1]
    peer_count = section_face.shape[1]
    capacity = section_face.shape[2]
    wanted = section_face[0].reshape(-1)
    picked = jnp.take(face_values, jnp.maximum(wanted, 0), axis=1)
    outgoing = jnp.where((wanted >= 0)[None, :], picked, 0.0).reshape(
        EDGE * EDGE, peer_count, capacity
    )
    own_index = lax.axis_index("gy")
    arrived = lax.all_to_all(outgoing, "gy", split_axis=1, concat_axis=1, tiled=True)
    swapped = arrived.reshape(EDGE * EDGE, peer_count, capacity // 2, 2)[..., ::-1].reshape(
        EDGE * EDGE, peer_count, capacity
    )
    arrived = jnp.where((jnp.arange(peer_count) == own_index)[None, :, None], swapped, arrived)
    incoming = orient_columns(
        arrived.reshape(EDGE * EDGE, peer_count * capacity), section_code[0].reshape(-1)
    )
    pipe_ids = pipe_face[0]
    pipe_width = pipe_ids.shape[1]
    boundary = jnp.take(face_values, pipe_ids.reshape(-1), axis=1).reshape(
        EDGE * EDGE, 2, pipe_width
    )
    extended = padded(boundary, (("gx", 1),), 1)
    beside = jnp.concatenate([extended[:, 0], extended[:, 3]], axis=1)
    beside = orient_columns(beside, pipe_code[0].reshape(-1))
    targets = jnp.concatenate([wanted, pipe_ids.reshape(-1)])
    placed = jnp.where(targets < 0, face_count, targets)
    face_extra = (
        jnp.zeros((EDGE * EDGE, face_count), jnp.float32)
        .at[:, placed]
        .add(jnp.concatenate([incoming, beside], axis=1), mode="drop")
    )
    face_parts = face_extra.reshape(EDGE, EDGE, slot_count, 6)
    element_cube = element_cube.at[0].add(face_parts[..., 0])
    element_cube = element_cube.at[EDGE - 1].add(face_parts[..., 1])
    element_cube = element_cube.at[:, 0].add(face_parts[..., 2])
    element_cube = element_cube.at[:, EDGE - 1].add(face_parts[..., 3])
    element_cube = element_cube.at[:, :, 0].add(face_parts[..., 4])
    element_cube = element_cube.at[:, :, EDGE - 1].add(face_parts[..., 5])
    return element_cube.reshape(EDGE**3, -1)


def on_device(
    solution,
    residual,
    metric_diag,
    metric_cross,
    fdm_vectors,
    fdm_values,
    vertex_ids,
    coarse_inverse,
    elem_live,
    section_face,
    section_code,
    pipe_face,
    pipe_code,
):
    slot_count = residual.shape[1]
    alive_mask = (jnp.arange(slot_count) < elem_live[0]).astype(jnp.float32)
    rmask = residual * alive_mask[None, :]
    corner_weights = corner_table()
    derivative = derivative_matrix()
    corners = jnp.dot(corner_weights, rmask, precision=top_precision)
    coarse_partial = jax.ops.segment_sum(
        corners.reshape(-1), vertex_ids.reshape(-1), num_segments=coarse_inverse.shape[1]
    )
    coarse_rhs = lax.psum(coarse_partial, ("gx", "gy"))
    own_values = jnp.dot(coarse_inverse, coarse_rhs, precision=top_precision)
    coarse_sol = lax.all_gather(own_values, ("gx", "gy"), axis=0, tiled=True)
    smooth = fdm_solve(rmask.reshape(EDGE, EDGE, EDGE, -1), fdm_vectors, fdm_values).reshape(
        EDGE**3, -1
    )
    summed = face_sum(smooth, section_face, section_code, pipe_face, pipe_code)
    lifted = jnp.dot(corner_weights.T, coarse_sol[vertex_ids], precision=top_precision)
    direction = alive_mask[None, :] * (summed + lifted)
    applied, curvature_local = local_operator(direction, metric_diag, metric_cross, derivative)
    image = face_sum(applied, section_face, section_code, pipe_face, pipe_code)
    precond_local = jnp.sum(rmask * direction)
    norm_local = jnp.sum(rmask * rmask)
    precond_dot, curvature, old_norm = lax.psum(
        (precond_local, curvature_local, norm_local), ("gx", "gy")
    )
    step_length = precond_dot / curvature
    residual_out = rmask - step_length * image
    fresh_norm = lax.psum(jnp.sum(residual_out * residual_out), ("gx", "gy"))
    solution_out = alive_mask[None, :] * (solution + step_length * direction)
    norm_ratio = (fresh_norm / old_norm).reshape(1)
    return (solution_out, residual_out, norm_ratio)


def solution(mesh):
    placed = (
        P(None, ("gx", "gy")),
        P(None, ("gx", "gy")),
        P(None, None, ("gx", "gy")),
        P(None, None, ("gx", "gy")),
        P(None, None, None, ("gx", "gy")),
        P(None, None, ("gx", "gy")),
        P(None, ("gx", "gy")),
        P(("gx", "gy"), None),
        P(("gx", "gy")),
        P(("gx", "gy"), None, None),
        P(("gx", "gy"), None, None),
        P(("gx", "gy"), None, None),
        P(("gx", "gy"), None, None),
    )
    return jax.shard_map(
        on_device,
        mesh=mesh,
        in_specs=placed,
        out_specs=(P(None, ("gx", "gy")), P(None, ("gx", "gy")), P()),
        check_vma=False,
    )
```

profile of v0, /device:TPU:1, one launch (start us, length us, event | category | flops | bytes accessed | tf_op | source)
XLA Modules:
  0.0 567.3 jit_solution(12377010773833954774)
XLA Ops:
  6.8 2.3 copy.389
  9.0 2.5 reshape.1869
  14.6 7.6 %all-to-all-start = ((f32[16,1,1280]{2,1,0:T(1,128)}), f32[16,1,1280]{2,1,0:T(1,128)}, u32[]{:S(2)}, u32[]{:S(2)}) async-start(f32[16,1,1280]{2,1,0:T(1,128)} %reshape.1990), calls=%async_computation | async-start | bytes 163840 | tf_op jit(solution)/shard_map/all_to_all | solution.py:137
  23.7 2.5 collective-permute-start
  30.1 5.9 %scatter_custom_fusion.1 = f32[8192]{0:T(1024)S(1)} fusion(s32[1024]{0:T(1024)S(1)} %bitcast.649, f32[1024]{0:T(1024)S(1)} %convolution_bitcast_fusion, f32[]{:T(128)} %constant.402.clone.1), kind=kCustom, calls=%fused_computation.199 | custom fusion | flops 1024 | bytes 32772 | tf_op jit(solution)/shard_map/scatter-add | solution.py:191
  36.1 108.5 %psum.35 = f32[8192]{0:T(1024)S(1)} all-reduce(f32[8192]{0:T(1024)S(1)} %scatter_custom_fusion.1), channel_id=1, replica_groups=mesh['gx'=32,'gy'=16] {'gx','gy'}, use_global_device_ids=true, to_apply=%region_2.5 | all-reduce | flops 8192 | bytes 65536 | tf_op jit(solution)/shard_map/psum | solution.py:194
  169.9 99.5 %all-reduce = f32[8192]{0:T(1024)S(1)} all-reduce(f32[8192]{0:T(1024)S(1)} %dynamic-update-slice.36), channel_id=1, replica_groups=mesh['gx'=32,'gy'=16] {'gx','gy'}, use_global_device_ids=true, to_apply=%add | all-reduce | flops 8192 | bytes 65536
  269.4 10.5 %gather_fusion = f32[1024]{0:T(1024)} fusion(f32[8192]{0:T(1024)S(1)} %all-reduce, s32[1024]{0:T(1024)S(1)} %fusion.40), kind=kCustom, calls=%fused_computation.4 | custom fusion | bytes 12288 | tf_op jit(solution)/shard_map/gather | solution.py:201
  280.6 1.6 reduce.26
  283.5 2.3 scatter_custom_fusion
  285.7 2.6 reshape.1876
  288.4 3.4 fusion.54
  291.8 1.9 copy.456
  294.4 1.3 copy.401
  295.7 1.2 copy.403
  298.1 1.2 copy.459
  301.8 2.0 multiply_reduce_fusion
  304.4 1.5 multiply_add_fusion
  306.1 1.5 add_bitcast_fusion.1
  309.7 2.3 copy.428
  312.0 2.4 reshape.1886
  317.3 4.2 all-to-all-start.1
  322.3 1.8 collective-permute-start.2
  339.6 2.9 add_reduce_fusion
  343.7 102.5 %all-reduce.2 = (f32[]{:T(128)}, f32[]{:T(128)}) all-reduce(f32[]{:T(128)} %get-tuple-element.150, f32[]{:T(128)S(6)} %add.970), channel_id=1, replica_groups=mesh['gx'=32,'gy'=16] {'gx','gy'}, use_global_device_ids=true, to_apply=%region_4.7 | all-reduce | flops 2 | bytes 16 | tf_op jit(solution)/shard_map/psum | solution.py:207
  447.6 1.7 add_multiply_fusion
  450.2 1.6 reduce.27
  453.1 2.5 scatter_custom_fusion.2
  455.7 2.6 reshape.1893
  458.3 2.9 fusion.53
  464.1 1.3 multiply_reduce_fusion.1
  465.4 99.4 %all-reduce.1 = (f32[]{:T(128)}, f32[]{:T(128)}) all-reduce(f32[]{:T(128)} %get-tuple-element.156, f32[]{:T(128)} %get-tuple-element.149), channel_id=1, replica_groups=mesh['gx'=32,'gy'=16] {'gx','gy'}, use_global_device_ids=true, to_apply=%region_11.14 | all-reduce | flops 2 | bytes 16 | tf_op jit(solution)/shard_map/psum | solution.py:212
  (515 shorter events, 70.4 us)
Async XLA Ops:
  0.6 147.6 %copy-start = (f32[16,8192]{1,0:T(8,128)S(1)}, f32[16,8192]{1,0:T(8,128)}, u32[]{:S(2)}) copy-start(f32[16,8192]{1,0:T(8,128)} %param.48) | copy-start | bytes 1572868
  9.0 21.1 %copy-start.121 = (s32[8,128]{1,0:T(8,128)S(1)}, s32[8,128]{1,0:T(8,128)}, u32[]{:S(2)}) copy-start(s32[8,128]{1,0:T(8,128)} %param.47) | copy-start | bytes 12292
  9.0 135.9 %copy-start.2 = (bf16[3,512,128]{2,1,0:T(8,128)(2,1)S(1)}, bf16[3,512,128]{2,1,0:T(8,128)(2,1)}, u32[]{:S(2)}) copy-start(bf16[3,512,128]{2,1,0:T(8,128)(2,1)} %param.44) | copy-start | bytes 1179652
  11.5 134.5 %copy-start.1 = (bf16[3,512,128]{2,1,0:T(8,128)(2,1)S(1)}, bf16[3,512,128]{2,1,0:T(8,128)(2,1)}, u32[]{:S(2)}) copy-start(bf16[3,512,128]{2,1,0:T(8,128)(2,1)} %param.43) | copy-start | bytes 1179652
  12.5 134.4 %copy-start.110 = (s32[1024]{0:T(1024)}, s32[1024]{0:T(1024)S(1)}, u32[]{:S(2)}) copy-start(s32[1024]{0:T(1024)S(1)} %get-tuple-element.373) | copy-start | bytes 12292
  14.6 265.5 %all-to-all-start = ((f32[16,1,1280]{2,1,0:T(1,128)}), f32[16,1,1280]{2,1,0:T(1,128)}, u32[]{:S(2)}, u32[]{:S(2)}) async-start(f32[16,1,1280]{2,1,0:T(1,128)} %reshape.1990), calls=%async_computation | async-start | bytes 163840 | tf_op jit(solution)/shard_map/all_to_all | solution.py:137
  23.5 256.5 %copy-start.66 = (pred[128]{0:T(512)(128)(4,1)}, pred[128]{0:T(512)(128)(4,1)S(1)}, u32[]{:S(2)}) copy-start(pred[128]{0:T(512)(128)(4,1)S(1)} %get-tuple-element.360) | copy-start | bytes 388
  23.7 256.2 %collective-permute-start = (f32[64,1,64]{2,0,1:T(8,128)S(1)}, f32[64,1,64]{2,0,1:T(8,128)S(1)}, u32[]{:S(2)}, u32[]{:S(2)}) collective-permute-start(f32[64,1,64]{2,0,1:T(8,128)S(1)} %copy.454), channel_id=1, source_target_pairs={{0,16},{16,32},{32,48},{48,64},{64,80},{80,96},{96,112},{112,128},... | collective-permute-start | bytes 49160 | tf_op jit(solution)/shard_map/ppermute | solution.py:16
  26.8 253.1 %collective-permute-start.1 = (f32[64,1,64]{2,0,1:T(8,128)}, f32[64,1,64]{2,0,1:T(8,128)S(1)}, u32[]{:S(2)}, u32[]{:S(2)}) collective-permute-start(f32[64,1,64]{2,0,1:T(8,128)} %copy.455), channel_id=1, source_target_pairs={{16,0},{32,16},{48,32},{64,48},{80,64},{96,80},{112,96},{128,112},... | collective-permute-start | bytes 49160 | tf_op jit(solution)/shard_map/ppermute | solution.py:19
  144.9 19.5 %copy-start.42 = (f32[8]{0:T(128)}, f32[8]{0:T(128)S(1)}, u32[]{:S(2)}) copy-start(f32[8]{0:T(128)S(1)} %get-tuple-element.346) | copy-start | bytes 100
  144.9 20.1 %copy-start.56 = (f32[8]{0:T(128)}, f32[8]{0:T(128)S(1)}, u32[]{:S(2)}) copy-start(f32[8]{0:T(128)S(1)} %get-tuple-element.353) | copy-start | bytes 100
  144.9 20.8 %copy-start.54 = (f32[8]{0:T(128)}, f32[8]{0:T(128)S(1)}, u32[]{:S(2)}) copy-start(f32[8]{0:T(128)S(1)} %get-tuple-element.352) | copy-start | bytes 100
  144.9 21.4 %copy-start.52 = (f32[8]{0:T(128)}, f32[8]{0:T(128)S(1)}, u32[]{:S(2)}) copy-start(f32[8]{0:T(128)S(1)} %get-tuple-element.351) | copy-start | bytes 100
  144.9 22.1 %copy-start.50 = (f32[8]{0:T(128)}, f32[8]{0:T(128)S(1)}, u32[]{:S(2)}) copy-start(f32[8]{0:T(128)S(1)} %get-tuple-element.350) | copy-start | bytes 100
  144.9 22.8 %copy-start.48 = (f32[8]{0:T(128)}, f32[8]{0:T(128)S(1)}, u32[]{:S(2)}) copy-start(f32[8]{0:T(128)S(1)} %get-tuple-element.349) | copy-start | bytes 100
  144.9 23.5 %copy-start.46 = (f32[8]{0:T(128)}, f32[8]{0:T(128)S(1)}, u32[]{:S(2)}) copy-start(f32[8]{0:T(128)S(1)} %get-tuple-element.348) | copy-start | bytes 100
  145.0 24.1 %copy-start.44 = (f32[8]{0:T(128)}, f32[8]{0:T(128)S(1)}, u32[]{:S(2)}) copy-start(f32[8]{0:T(128)S(1)} %get-tuple-element.347) | copy-start | bytes 100
  152.5 127.5 %copy-start.83 = (pred[128]{0:T(512)(128)(4,1)S(1)}, pred[128]{0:T(512)(128)(4,1)}, u32[]{:S(2)}) copy-start(pred[128]{0:T(512)(128)(4,1)} %get-tuple-element.361) | copy-start | bytes 388
  152.6 127.5 %copy-start.117 = (pred[128]{0:T(512)(128)(4,1)S(1)}, pred[128]{0:T(512)(128)(4,1)}, u32[]{:S(2)}) copy-start(pred[128]{0:T(512)(128)(4,1)} %get-tuple-element.359) | copy-start | bytes 388
  165.0 117.4 %copy-start.122 = (pred[16]{0:T(512)(128)(4,1)S(1)}, pred[16]{0:T(512)(128)(4,1)}, u32[]{:S(2)}) copy-start(pred[16]{0:T(512)(128)(4,1)} %iota_compare_fusion.2) | copy-start | bytes 52
  317.3 132.9 %all-to-all-start.1 = ((f32[16,1,1280]{2,1,0:T(1,128)}), f32[16,1,1280]{2,1,0:T(1,128)}, u32[]{:S(2)}, u32[]{:S(2)}) async-start(f32[16,1,1280]{2,1,0:T(1,128)} %reshape.1992), calls=%async_computation.1 | async-start | bytes 163840 | tf_op jit(solution)/shard_map/all_to_all | solution.py:137
  321.4 17.7 %copy-start.19 = (f32[1,8,8,128]{3,0,2,1:T(1,128)S(1)}, f32[1,8,8,128]{3,0,2,1:T(1,128)}, u32[]{:S(2)}) copy-start(f32[1,8,8,128]{3,0,2,1:T(1,128)} %copy-done.18) | copy-start | bytes 98308
  322.3 127.0 %collective-permute-start.2 = (f32[64,1,64]{2,0,1:T(8,128)}, f32[64,1,64]{2,0,1:T(8,128)}, u32[]{:S(2)}, u32[]{:S(2)}) collective-permute-start(f32[64,1,64]{2,0,1:T(8,128)} %copy.460), channel_id=1, source_target_pairs={{0,16},{16,32},{32,48},{48,64},{64,80},{80,96},{96,112},{112,128},... | collective-permute-start | bytes 49160 | tf_op jit(solution)/shard_map/ppermute | solution.py:16
  324.8 124.5 %collective-permute-start.3 = (f32[64,1,64]{2,0,1:T(8,128)}, f32[64,1,64]{2,0,1:T(8,128)}, u32[]{:S(2)}, u32[]{:S(2)}) collective-permute-start(f32[64,1,64]{2,0,1:T(8,128)} %copy.461), channel_id=1, source_target_pairs={{16,0},{32,16},{48,32},{64,48},{80,64},{96,80},{112,96},{128,112},... | collective-permute-start | bytes 49160 | tf_op jit(solution)/shard_map/ppermute | solution.py:19
  339.5 108.0 %copy-start.72 = (f32[128]{0:T(128)S(1)}, f32[128]{0:T(128)}, u32[]{:S(2)}) copy-start(f32[128]{0:T(128)} %copy-done.71) | copy-start | bytes 1540
  339.5 110.6 %copy-start.67 = (pred[128]{0:T(512)(128)(4,1)S(1)}, pred[128]{0:T(512)(128)(4,1)}, u32[]{:S(2)}) copy-start(pred[128]{0:T(512)(128)(4,1)} %copy-done.66) | copy-start | bytes 388
  339.6 110.6 %copy-start.84 = (pred[128]{0:T(512)(128)(4,1)S(1)}, pred[128]{0:T(512)(128)(4,1)}, u32[]{:S(2)}) copy-start(pred[128]{0:T(512)(128)(4,1)} %get-tuple-element.361) | copy-start | bytes 388
  339.6 110.6 %copy-start.118 = (pred[128]{0:T(512)(128)(4,1)S(1)}, pred[128]{0:T(512)(128)(4,1)}, u32[]{:S(2)}) copy-start(pred[128]{0:T(512)(128)(4,1)} %get-tuple-element.359) | copy-start | bytes 388
  339.6 112.4 %copy-start.123 = (pred[16]{0:T(512)(128)(4,1)S(1)}, pred[16]{0:T(512)(128)(4,1)}, u32[]{:S(2)}) copy-start(pred[16]{0:T(512)(128)(4,1)} %iota_compare_fusion.2) | copy-start | bytes 52
  342.5 110.2 %copy-start.65 = (pred[320]{0:T(512)(128)(4,1)S(1)}, pred[320]{0:T(512)(128)(4,1)}, u32[]{:S(2)}) copy-start(pred[320]{0:T(512)(128)(4,1)} %get-tuple-element.355) | copy-start | bytes 964
  342.5 110.4 %copy-start.74 = (pred[320]{0:T(512)(128)(4,1)S(1)}, pred[320]{0:T(512)(128)(4,1)}, u32[]{:S(2)}) copy-start(pred[320]{0:T(512)(128)(4,1)} %get-tuple-element.356) | copy-start | bytes 964
  342.5 110.4 %copy-start.112 = (pred[320]{0:T(512)(128)(4,1)S(1)}, pred[320]{0:T(512)(128)(4,1)}, u32[]{:S(2)}) copy-start(pred[320]{0:T(512)(128)(4,1)} %get-tuple-element.354) | copy-start | bytes 964
  (100 other events, 699.8 us)
where the time goes:
time: 570 us; the launch traced here: 567 us
  blocking collectives  410 us (72%)
  local copies, waits for them, and re-layouts  94 us (16%)
  other arithmetic  34.3 us (6%)
  starting transfers between devices  17 us (3%)
  between operations  9.18 us (2%)
    psum x1, blocking collectives, on_device(): coarse_rhs = lax.psum(coarse_partial, ('gx', 'gy'))  109 us
    psum x1, blocking collectives, on_device(): lax.psum((precond_local, curvature_local, norm_local), ('gx', 'gy'))  102 us
    unnamed x1, blocking collectives  99.5 us
    psum x1, blocking collectives, on_device(): fresh_norm = lax.psum(jnp.sum(residual_out * residual_out), ('gx', 'gy'))  99.4 us
    mul x78, local copies, waits for them, and re-layouts, contract(): total = total + matrices[index][:, None, None, :] * moved[index][None]  28.3 us
    unnamed x280, local copies, waits for them, and re-layouts  12 us
    all_to_all x2, starting transfers between devices, face_sum(): lax.all_to_all(outgoing, 'gy', split_axis=1, concat_axis=1, tiled=True)  11.8 us
  transfers between devices with their start and end apart: 6, of which 0 were waited for; matrix products, arithmetic and copies ran while one was open for 12% of the time, Pallas kernels for 0%

commit v1 on v0

--- a/solution.py
+++ b/solution.py
@@ -191,7 +191,7 @@
     coarse_partial = jax.ops.segment_sum(
         corners.reshape(-1), vertex_ids.reshape(-1), num_segments=coarse_inverse.shape[1]
     )
-    coarse_rhs = lax.psum(coarse_partial, ("gx", "gy"))
+    coarse_rhs = jnp.sum(lax.all_gather(coarse_partial, axis_name=("gx", "gy")), 0)
     own_values = jnp.dot(coarse_inverse, coarse_rhs, precision=top_precision)
     coarse_sol = lax.all_gather(own_values, ("gx", "gy"), axis=0, tiled=True)
     smooth = fdm_solve(rmask.reshape(EDGE, EDGE, EDGE, -1), fdm_vectors, fdm_values).reshape(

time: 570 us -> 650 us (1.14)
  waiting for transfers between devices: 0.02 us -> 152 us
  blocking collectives: 410 us -> 304 us
  local copies, waits for them, and re-layouts: 94 us -> 108 us
  between operations: 9.18 us -> 22.7 us
    all_gather x0 -> x1, waiting for transfers between devices: none -> 152 us  [on_device(): lax.all_gather(coarse_partial, axis_name=('gx', 'gy'))]
    psum x1 -> x0, blocking collectives: 109 us -> none  [on_device(): coarse_rhs = lax.psum(coarse_partial, ('gx', 'gy'))]
    all_gather x0 -> x1, local copies, waits for them, and re-layouts: none -> 18.2 us  [on_device(): lax.all_gather(coarse_partial, axis_name=('gx', 'gy'))]
    reduce_sum x0 -> x1, other arithmetic: none -> 6.55 us  [on_device(): jnp.sum(lax.all_gather(coarse_partial, axis_name=('gx', 'gy')), 0)]
  transfers between devices with their start and end apart: 6 -> 7, of which waited for: 0 -> 1; matrix products, arithmetic and copies ran while one was open for 12% -> 13% of each run, Pallas kernels for 0% -> 0%
where the time goes in v1:
time: 650 us; the launch traced here: 647 us
  blocking collectives  304 us (47%)
  waiting for transfers between devices  152 us (23%)
  local copies, waits for them, and re-layouts  108 us (17%)
  other arithmetic  40.2 us (6%)
  between operations  22.7 us (3%)
  starting transfers between devices  16.5 us (3%)
    all_gather x1, waiting for transfers between devices, on_device(): lax.all_gather(coarse_partial, axis_name=('gx', 'gy'))  152 us
    psum x1, blocking collectives, on_device(): lax.psum((precond_local, curvature_local, norm_local), ('gx', 'gy'))  103 us
    unnamed x1, blocking collectives  101 us
    psum x1, blocking collectives, on_device(): fresh_norm = lax.psum(jnp.sum(residual_out * residual_out), ('gx', 'gy'))  99.4 us
    mul x78, local copies, waits for them, and re-layouts, contract(): total = total + matrices[index][:, None, None, :] * moved[index][None]  28.6 us
    all_gather x1, local copies, waits for them, and re-layouts, on_device(): lax.all_gather(coarse_partial, axis_name=('gx', 'gy'))  18.2 us
  transfers between devices with their start and end apart: 7, of which 1 were waited for; matrix products, arithmetic and copies ran while one was open for 13% of the time, Pallas kernels for 0%

profile of v1, /device:TPU:1, one launch (start us, length us, event | category | flops | bytes accessed | tf_op | source)
XLA Modules:
  0.0 646.7 jit_solution(8673974330292471463)
XLA Ops:
  9.6 6.6 %scatter_custom_fusion.1 = f32[8192]{0:T(1024)} fusion(s32[1024]{0:T(1024)} %bitcast.649, f32[1024]{0:T(1024)S(1)} %convolution_bitcast_fusion, f32[]{:T(128)} %constant.402.clone.1), kind=kCustom, calls=%fused_computation.199 | custom fusion | flops 1024 | bytes 33280 | tf_op jit(solution)/shard_map/scatter-add | solution.py:191
  21.4 2.3 copy.389
  23.7 2.5 reshape.1869
  29.9 7.6 %all-to-all-start = ((f32[16,1,1280]{2,1,0:T(1,128)}), f32[16,1,1280]{2,1,0:T(1,128)}, u32[]{:S(2)}, u32[]{:S(2)}) async-start(f32[16,1,1280]{2,1,0:T(1,128)} %reshape.1991), calls=%async_computation | async-start | bytes 163840 | tf_op jit(solution)/shard_map/all_to_all | solution.py:137
  38.5 2.5 collective-permute-start
  69.6 1.7 reduce.26
  72.5 2.5 scatter_custom_fusion
  75.0 2.6 reshape.1876
  77.6 3.4 fusion.54
  81.1 1.2 copy.456
  82.3 1.2 copy.457
  83.5 1.2 copy.401
  84.8 1.2 copy.403
  89.6 152.3 %all-gather.3.cloned.1.call-done = f32[4194304]{0:T(1024)} async-done(((f32[8192]{0:T(1024)}), f32[4194304]{0:T(1024)}) %all-gather.3.cloned.1.call-update) | async-done | bytes 16777232 | tf_op jit(solution)/shard_map/all_gather | solution.py:194
  241.9 18.2 %reshape.1965 = f32[512,8192]{1,0:T(8,128)} reshape(f32[4194304]{0:T(1024)} %all-gather.3.cloned.1.call-done) | data formatting | bytes 33554432 | tf_op jit(solution)/shard_map/all_gather | solution.py:194
  260.2 6.5 %reduce_sum.63 = f32[8192]{0:T(1024)S(1)} reduce(f32[512,8192]{1,0:T(8,128)} %reshape.1965, f32[]{:T(128)} %constant.402.clone.1), dimensions={0}, to_apply=%region_2.5 | reduce | flops 4186112 | bytes 16809988 | tf_op jit(solution)/shard_map/reduce_sum | solution.py:194
  267.7 101.2 %all-reduce = f32[8192]{0:T(1024)S(1)} all-reduce(f32[8192]{0:T(1024)S(1)} %dynamic-update-slice.36), channel_id=1, replica_groups=mesh['gx'=32,'gy'=16] {'gx','gy'}, use_global_device_ids=true, to_apply=%add | all-reduce | flops 8192 | bytes 65536
  368.9 6.2 gather_fusion
  375.2 2.3 multiply_reduce_fusion
  378.0 1.7 multiply_add_fusion
  382.7 2.3 copy.428
  385.0 2.4 reshape.1886
  390.3 4.4 all-to-all-start.1
  412.0 2.9 add_reduce_fusion
  416.2 103.0 %all-reduce.2 = (f32[]{:T(128)}, f32[]{:T(128)}) all-reduce(f32[]{:T(128)} %get-tuple-element.150, f32[]{:T(128)S(6)} %add.968), channel_id=1, replica_groups=mesh['gx'=32,'gy'=16] {'gx','gy'}, use_global_device_ids=true, to_apply=%region_4.7 | all-reduce | flops 2 | bytes 16 | tf_op jit(solution)/shard_map/psum | solution.py:207
  520.4 1.7 add_multiply_fusion
  523.1 1.7 reduce.27
  526.0 2.3 scatter_custom_fusion.2
  528.3 2.6 reshape.1893
  530.9 2.9 fusion.53
  536.7 1.3 multiply_reduce_fusion.1
  538.1 99.4 %all-reduce.1 = (f32[]{:T(128)}, f32[]{:T(128)}) all-reduce(f32[]{:T(128)} %get-tuple-element.156, f32[]{:T(128)} %get-tuple-element.149), channel_id=1, replica_groups=mesh['gx'=32,'gy'=16] {'gx','gy'}, use_global_device_ids=true, to_apply=%region_11.14 | all-reduce | flops 2 | bytes 16 | tf_op jit(solution)/shard_map/psum | solution.py:212
  (539 shorter events, 72.3 us)
Async XLA Ops:
  7.2 259.6 %copy-start = (f32[16,8192]{1,0:T(8,128)S(1)}, f32[16,8192]{1,0:T(8,128)}, u32[]{:S(2)}) copy-start(f32[16,8192]{1,0:T(8,128)} %param.48) | copy-start | bytes 1572868
  7.2 234.8 %all-gather.3.cloned.1.call-start = ((), (), s32[]{:S(2)}) async-start(), calls=%async_computation.2 | async-start | bytes 16809984 | tf_op jit(solution)/shard_map/all_gather | solution.py:194
  23.7 22.2 %copy-start.2 = (bf16[3,512,128]{2,1,0:T(8,128)(2,1)S(1)}, bf16[3,512,128]{2,1,0:T(8,128)(2,1)}, u32[]{:S(2)}) copy-start(bf16[3,512,128]{2,1,0:T(8,128)(2,1)} %param.44) | copy-start | bytes 1179652
  26.2 20.7 %copy-start.1 = (bf16[3,512,128]{2,1,0:T(8,128)(2,1)S(1)}, bf16[3,512,128]{2,1,0:T(8,128)(2,1)}, u32[]{:S(2)}) copy-start(bf16[3,512,128]{2,1,0:T(8,128)(2,1)} %param.43) | copy-start | bytes 1179652
  26.6 21.2 %copy-start.120 = (s32[1024]{0:T(1024)}, s32[1024]{0:T(1024)S(1)}, u32[]{:S(2)}) copy-start(s32[1024]{0:T(1024)S(1)} %get-tuple-element.373) | copy-start | bytes 12292
  29.9 39.1 %all-to-all-start = ((f32[16,1,1280]{2,1,0:T(1,128)}), f32[16,1,1280]{2,1,0:T(1,128)}, u32[]{:S(2)}, u32[]{:S(2)}) async-start(f32[16,1,1280]{2,1,0:T(1,128)} %reshape.1991), calls=%async_computation | async-start | bytes 163840 | tf_op jit(solution)/shard_map/all_to_all | solution.py:137
  38.3 30.7 %copy-start.70 = (pred[128]{0:T(512)(128)(4,1)}, pred[128]{0:T(512)(128)(4,1)S(1)}, u32[]{:S(2)}) copy-start(pred[128]{0:T(512)(128)(4,1)S(1)} %get-tuple-element.360) | copy-start | bytes 388
  38.3 30.7 %copy-start.93 = (pred[128]{0:T(512)(128)(4,1)}, pred[128]{0:T(512)(128)(4,1)S(1)}, u32[]{:S(2)}) copy-start(pred[128]{0:T(512)(128)(4,1)S(1)} %get-tuple-element.361) | copy-start | bytes 388
  38.3 30.7 %copy-start.127 = (pred[128]{0:T(512)(128)(4,1)}, pred[128]{0:T(512)(128)(4,1)S(1)}, u32[]{:S(2)}) copy-start(pred[128]{0:T(512)(128)(4,1)S(1)} %get-tuple-element.359) | copy-start | bytes 388
  38.5 30.3 %collective-permute-start = (f32[64,1,64]{2,0,1:T(8,128)S(1)}, f32[64,1,64]{2,0,1:T(8,128)S(1)}, u32[]{:S(2)}, u32[]{:S(2)}) collective-permute-start(f32[64,1,64]{2,0,1:T(8,128)S(1)} %copy.454), channel_id=1, source_target_pairs={{0,16},{16,32},{32,48},{48,64},{64,80},{80,96},{96,112},{112,128},... | collective-permute-start | bytes 49160 | tf_op jit(solution)/shard_map/ppermute | solution.py:16
  41.1 27.8 %collective-permute-start.1 = (f32[64,1,64]{2,0,1:T(8,128)S(1)}, f32[64,1,64]{2,0,1:T(8,128)S(1)}, u32[]{:S(2)}, u32[]{:S(2)}) collective-permute-start(f32[64,1,64]{2,0,1:T(8,128)S(1)} %copy.455), channel_id=1, source_target_pairs={{16,0},{32,16},{48,32},{64,48},{80,64},{96,80},{112,96},{128,112},... | collective-permute-start | bytes 49160 | tf_op jit(solution)/shard_map/ppermute | solution.py:19
  43.8 20.9 %copy-start.53 = (f32[8]{0:T(128)}, f32[8]{0:T(128)S(1)}, u32[]{:S(2)}) copy-start(f32[8]{0:T(128)S(1)} %get-tuple-element.352) | copy-start | bytes 100
  43.8 21.6 %copy-start.51 = (f32[8]{0:T(128)}, f32[8]{0:T(128)S(1)}, u32[]{:S(2)}) copy-start(f32[8]{0:T(128)S(1)} %get-tuple-element.351) | copy-start | bytes 100
  43.8 22.3 %copy-start.49 = (f32[8]{0:T(128)}, f32[8]{0:T(128)S(1)}, u32[]{:S(2)}) copy-start(f32[8]{0:T(128)S(1)} %get-tuple-element.350) | copy-start | bytes 100
  43.8 22.9 %copy-start.47 = (f32[8]{0:T(128)}, f32[8]{0:T(128)S(1)}, u32[]{:S(2)}) copy-start(f32[8]{0:T(128)S(1)} %get-tuple-element.349) | copy-start | bytes 100
  43.8 23.6 %copy-start.45 = (f32[8]{0:T(128)}, f32[8]{0:T(128)S(1)}, u32[]{:S(2)}) copy-start(f32[8]{0:T(128)S(1)} %get-tuple-element.348) | copy-start | bytes 100
  43.9 24.3 %copy-start.43 = (f32[8]{0:T(128)}, f32[8]{0:T(128)S(1)}, u32[]{:S(2)}) copy-start(f32[8]{0:T(128)S(1)} %get-tuple-element.347) | copy-start | bytes 100
  51.5 20.8 %copy-start.83 = (pred[320]{0:T(512)(128)(4,1)S(1)}, pred[320]{0:T(512)(128)(4,1)}, u32[]{:S(2)}) copy-start(pred[320]{0:T(512)(128)(4,1)} %get-tuple-element.356) | copy-start | bytes 964
  51.5 20.8 %copy-start.121 = (pred[320]{0:T(512)(128)(4,1)S(1)}, pred[320]{0:T(512)(128)(4,1)}, u32[]{:S(2)}) copy-start(pred[320]{0:T(512)(128)(4,1)} %get-tuple-element.354) | copy-start | bytes 964
  260.2 108.7 %copy-start.79 = (s32[1024]{0:T(1024)S(1)}, s32[1024]{0:T(1024)}, u32[]{:S(2)}) copy-start(s32[1024]{0:T(1024)} %fusion.40) | copy-start | bytes 12292
  266.7 108.4 %copy-start.81 = (f32[128]{0:T(128)S(1)}, f32[128]{0:T(128)}, u32[]{:S(2)}) copy-start(f32[128]{0:T(128)} %copy-done.80) | copy-start | bytes 1540
  390.3 132.8 %all-to-all-start.1 = ((f32[16,1,1280]{2,1,0:T(1,128)}), f32[16,1,1280]{2,1,0:T(1,128)}, u32[]{:S(2)}, u32[]{:S(2)}) async-start(f32[16,1,1280]{2,1,0:T(1,128)} %reshape.1993), calls=%async_computation.1 | async-start | bytes 163840 | tf_op jit(solution)/shard_map/all_to_all | solution.py:137
  395.5 126.6 %collective-permute-start.2 = (f32[64,1,64]{2,0,1:T(8,128)}, f32[64,1,64]{2,0,1:T(8,128)}, u32[]{:S(2)}, u32[]{:S(2)}) collective-permute-start(f32[64,1,64]{2,0,1:T(8,128)} %copy.460), channel_id=1, source_target_pairs={{0,16},{16,32},{32,48},{48,64},{64,80},{80,96},{96,112},{112,128},... | collective-permute-start | bytes 49160 | tf_op jit(solution)/shard_map/ppermute | solution.py:16
  397.2 124.9 %collective-permute-start.3 = (f32[64,1,64]{2,0,1:T(8,128)}, f32[64,1,64]{2,0,1:T(8,128)}, u32[]{:S(2)}, u32[]{:S(2)}) collective-permute-start(f32[64,1,64]{2,0,1:T(8,128)} %copy.461), channel_id=1, source_target_pairs={{16,0},{32,16},{48,32},{64,48},{80,64},{96,80},{112,96},{128,112},... | collective-permute-start | bytes 49160 | tf_op jit(solution)/shard_map/ppermute | solution.py:19
  412.0 108.4 %copy-start.82 = (f32[128]{0:T(128)S(1)}, f32[128]{0:T(128)}, u32[]{:S(2)}) copy-start(f32[128]{0:T(128)} %copy-done.80) | copy-start | bytes 1540
  412.0 111.0 %copy-start.71 = (pred[128]{0:T(512)(128)(4,1)S(1)}, pred[128]{0:T(512)(128)(4,1)}, u32[]{:S(2)}) copy-start(pred[128]{0:T(512)(128)(4,1)} %copy-done.70) | copy-start | bytes 388
  412.0 111.0 %copy-start.94 = (pred[128]{0:T(512)(128)(4,1)S(1)}, pred[128]{0:T(512)(128)(4,1)}, u32[]{:S(2)}) copy-start(pred[128]{0:T(512)(128)(4,1)} %copy-done.93) | copy-start | bytes 388
  412.0 111.0 %copy-start.128 = (pred[128]{0:T(512)(128)(4,1)S(1)}, pred[128]{0:T(512)(128)(4,1)}, u32[]{:S(2)}) copy-start(pred[128]{0:T(512)(128)(4,1)} %copy-done.127) | copy-start | bytes 388
  412.0 112.9 %copy-start.133 = (pred[16]{0:T(512)(128)(4,1)S(1)}, pred[16]{0:T(512)(128)(4,1)}, u32[]{:S(2)}) copy-start(pred[16]{0:T(512)(128)(4,1)} %iota_compare_fusion.2) | copy-start | bytes 52
  414.9 110.7 %copy-start.69 = (pred[320]{0:T(512)(128)(4,1)S(1)}, pred[320]{0:T(512)(128)(4,1)}, u32[]{:S(2)}) copy-start(pred[320]{0:T(512)(128)(4,1)} %get-tuple-element.355) | copy-start | bytes 964
  414.9 110.9 %copy-start.84 = (pred[320]{0:T(512)(128)(4,1)S(1)}, pred[320]{0:T(512)(128)(4,1)}, u32[]{:S(2)}) copy-start(pred[320]{0:T(512)(128)(4,1)} %get-tuple-element.356) | copy-start | bytes 964
  414.9 110.9 %copy-start.122 = (pred[320]{0:T(512)(128)(4,1)S(1)}, pred[320]{0:T(512)(128)(4,1)}, u32[]{:S(2)}) copy-start(pred[320]{0:T(512)(128)(4,1)} %get-tuple-element.354) | copy-start | bytes 964
  (111 other events, 832.6 us)
Sparse Core Ops, SparseCore 0:
  16.4 225.5 all-gather.2
